TPU v7x, 32 devices: a whole 2x2x4 slice. The times are simulated.
32 devices in a mesh: rep: 8 (over z, x), tp: 4 (over y, core).
Axes of the slice: x: 2, y: 2, z: 4, core: 2. Of those that a mesh axis runs over, the one named last changes fastest.
Arguments:
- hidden: bfloat16 [16384, 8192], P('rep', 'tp'), may hold values from -0.0625 to 0.0625
- target: bfloat16 [16384, 1024], P('rep'), may hold values from -6 to 6
- inner_weight: bfloat16 [8, 8192, 1024], P('rep', 'tp'), as said below
- first_moment: float32 [8, 8192, 1024], P('rep', 'tp'), may hold values from -1.5 to 1.5
- second_moment: float32 [8, 8192, 1024], P('rep', 'tp'), may hold values from 0.001 to 0.01
- anchor: float32 [4, 2048, 1024], P('tp', 'rep')
- outer_momentum: float32 [4, 2048, 1024], P('tp', 'rep'), may hold values from -1.5 to 1.5
Outputs:
- fragment: bfloat16 [8192, 1024], P('tp')
- momentum_new: float32 [4, 2048, 1024], P('tp', 'rep')
Inputs may be any that keep to these rules, and one draw needn't show every extreme that they name: `inner_weight`: each replica's inner weights are the anchor plus a drift of their own.
All inputs are finite; a program needn't handle non-finite values.
Results may differ from a plain program's by a relative error of at most 0.0017.
Values may be sent and summed in bfloat16 or wider, within the bound.
A program may use at most 128 MiB of HBM per device.

v0:
```python
import jax
import jax.numpy as jnp
from jax import lax
from jax.sharding import PartitionSpec as P

beta_one = 0.9
beta_two = 0.999
inner_rate = 0.2
decay_rate = 0.1
outer_rate = 0.7
outer_mu = 0.9
adam_eps = 1e-08


def local(hidden, target, inner_weight, first_moment, second_moment, anchor, outer_momentum):
    weight = inner_weight[0]
    partial_value = jnp.dot(hidden, weight, preferred_element_type=jnp.float32)
    summed = lax.psum_scatter(
        partial_value.astype(jnp.bfloat16), "tp", scatter_dimension=0, tiled=True
    ).astype(jnp.float32)
    count = summed.shape[0]
    goal = lax.dynamic_slice_in_dim(target, lax.axis_index("tp") * count, count, 0)
    residual = (summed - goal.astype(jnp.float32)).astype(jnp.bfloat16)
    grad = lax.dot_general(
        hidden,
        lax.all_gather(residual, "tp", axis=0, tiled=True),
        (((0,), (0,)), ((), ())),
        preferred_element_type=jnp.float32,
    )
    moment_one = beta_one * first_moment[0] + (1.0 - beta_one) * grad
    moment_two = beta_two * second_moment[0] + (1.0 - beta_two) * grad * grad
    corr_one = 1.0 - beta_one**3
    corr_two = 1.0 - beta_two**3
    weight_f = weight.astype(jnp.float32)
    step_dir = moment_one / corr_one / (jnp.sqrt(moment_two / corr_two) + adam_eps)
    updated = weight_f - inner_rate * (step_dir + decay_rate * weight_f)
    replicas = lax.axis_size("rep")
    replica_mean = lax.psum_scatter(updated, "rep", scatter_dimension=0, tiled=True) / replicas
    anchor_rows = anchor[0]
    delta = anchor_rows - replica_mean
    momentum_new = outer_mu * outer_momentum[0] + delta
    piece = (anchor_rows - outer_rate * (delta + outer_mu * momentum_new)).astype(jnp.bfloat16)
    fragment = lax.all_gather(piece, "rep", axis=0, tiled=True)
    return (fragment, momentum_new[None])


def solution(mesh):
    placed = (
        P("rep", "tp"),
        P("rep", None),
        P("rep", "tp", None),
        P("rep", "tp", None),
        P("rep", "tp", None),
        P("tp", "rep", None),
        P("tp", "rep", None),
    )
    return jax.shard_map(
        local,
        mesh=mesh,
        in_specs=placed,
        out_specs=(P("tp", None), P("tp", "rep", None)),
        check_vma=False,
    )
```

profile of v0, /device:TPU:0, one launch (start us, length us, event | category | flops | bytes accessed | tf_op | source)
XLA Modules:
  0.0 369.9 jit_solution(11761766374955327925)
XLA Ops:
  7.2 0.0 reduce-scatter.3.cloned.1.call-start
  7.2 13.8 %fusion.11 = bf16[2048,1024]{1,0:T(8,128)(2,1)} fusion(bf16[2048,2048]{1,0:T(8,128)(2,1)} %param.7, bf16[1,2048,1024]{2,1,0:T(8,128)(2,1)} %param.9), kind=kOutput, calls=%fused_computation.15 | convolution fusion | flops 8592031744 | bytes 16777216 | tf_op jit(solution)/shard_map/dot_general | solution.py:17
  21.0 0.0 reduce-scatter.3.cloned.1.call-update
  21.0 0.0 all-gather.3.cloned.1.call-start
  21.1 47.3 %reduce-scatter.3.cloned.1.call-done = bf16[512,1024]{1,0:T(8,128)(2,1)} async-done(((bf16[2048,1024]{1,0:T(8,128)(2,1)}), bf16[512,1024]{1,0:T(8,128)(2,1)}) %reduce-scatter.3.cloned.1.call-update) | async-done | bytes 1048592 | tf_op jit(solution)/shard_map/reduce_scatter | solution.py:18
  68.4 2.9 subtract_convert_fusion
  71.3 0.0 all-gather.3.cloned.1.call-update
  71.3 0.2 reduce-scatter.5.cloned.1.call-start
  71.6 6.4 %copy.10 = bf16[1,2048,1024]{1,2,0:T(8,128)(2,1)} copy(bf16[1,2048,1024]{2,1,0:T(8,128)(2,1)} %param.9) | data formatting | bytes 8388608 | tf_op args[2]
  78.0 9.5 %copy.11 = f32[1,2048,1024]{1,2,0:T(8,128)} copy(f32[1,2048,1024]{2,1,0:T(8,128)} %param.10) | data formatting | bytes 16777216 | tf_op args[3]
  87.5 9.2 %copy.12 = f32[1,2048,1024]{1,2,0:T(8,128)} copy(f32[1,2048,1024]{2,1,0:T(8,128)} %param.11) | data formatting | bytes 16777216 | tf_op args[4]
  96.7 9.3 %all-gather.3.cloned.1.call-done = bf16[2048,1024]{1,0:T(8,128)(2,1)} async-done(((bf16[512,1024]{1,0:T(8,128)(2,1)}), bf16[2048,1024]{1,0:T(8,128)(2,1)}) %all-gather.3.cloned.1.call-update) | async-done | bytes 4194320 | tf_op jit(solution)/shard_map/all_gather | solution.py:26
  106.0 24.9 %convert_subtract_fusion = f32[2048,1024]{0,1:T(8,128)} fusion(f32[1,2048,1024]{1,2,0:T(8,128)} %copy.12, f32[1,2048,1024]{1,2,0:T(8,128)} %copy.11, bf16[1,2048,1024]{1,2,0:T(8,128)(2,1)} %copy.10, bf16[2048,1024]{1,0:T(8,128)(2,1)} %all-gather.3.cloned.1.call-done, bf16[2048,2048]{1,0:T(8,128)(2,1)} %param.7), kind=kOutput, calls=%fused_computation.1 | convolution fusion | flops 8623489024 | bytes 41943040 | tf_op jit(solution)/shard_map/dot_general | solution.py:24
  130.8 0.0 copy-start
  130.8 0.0 reduce-scatter.5.cloned.1.call-update
  130.9 0.0 all-gather.5.cloned.1.call-start
  130.9 1.1 copy-done
  132.1 0.3 copy.13
  132.4 1.6 copy.9
  134.0 146.5 %reduce-scatter.5.cloned.1.call-done = f32[256,1024]{0,1:T(8,128)} async-done(((f32[2048,1024]{0,1:T(8,128)}), f32[256,1024]{0,1:T(8,128)}) %reduce-scatter.5.cloned.1.call-update) | async-done | bytes 1048592 | tf_op jit(solution)/shard_map/reduce_scatter | solution.py:38
  280.4 2.3 fusion.15
  282.8 0.0 all-gather.5.cloned.1.call-update
  282.8 1.3 copy.15
  284.1 72.9 %all-gather.5.cloned.1.call-done = bf16[2048,1024]{0,1:T(8,128)(2,1)} async-done(((bf16[256,1024]{0,1:T(8,128)(2,1)}), bf16[2048,1024]{0,1:T(8,128)(2,1)}) %all-gather.5.cloned.1.call-update) | async-done | bytes 4194320 | tf_op jit(solution)/shard_map/all_gather | solution.py:43
  357.0 6.4 %copy.14 = bf16[2048,1024]{1,0:T(8,128)(2,1)} copy(bf16[2048,1024]{0,1:T(8,128)(2,1)} %all-gather.5.cloned.1.call-done) | data formatting | bytes 8388608
Async XLA Ops:
  7.2 61.2 %reduce-scatter.3.cloned.1.call-start = ((), (), s32[]{:S(2)}) async-start(), calls=%async_computation.2 | async-start | bytes 5242880 | tf_op jit(solution)/shard_map/reduce_scatter | solution.py:18
  21.0 85.0 %all-gather.3.cloned.1.call-start = ((), (), s32[]{:S(2)}) async-start(), calls=%async_computation.3 | async-start | bytes 5242880 | tf_op jit(solution)/shard_map/all_gather | solution.py:26
  71.3 209.1 %reduce-scatter.5.cloned.1.call-start = ((), (), s32[]{:S(2)}) async-start(), calls=%async_computation.4 | async-start | bytes 9437184 | tf_op jit(solution)/shard_map/reduce_scatter | solution.py:38
  130.8 1.2 copy-start
  130.9 226.1 %all-gather.5.cloned.1.call-start = ((), (), s32[]{:S(2)}) async-start(), calls=%async_computation.5 | async-start | bytes 4718592 | tf_op jit(solution)/shard_map/all_gather | solution.py:43
Sparse Core Ops, SparseCore 0:
  21.1 47.2 reduce-scatter.2
  71.5 34.4 all-gather.2
  131.0 149.4 reduce-scatter.4
  282.9 73.9 all-gather.4
where the time goes:
time: 371 us; the launch traced here: 370 us
  waiting for transfers between devices  276 us (74%)
  matrix products  38.6 us (10%)
  local copies, waits for them, and re-layouts  35.8 us (10%)
  between operations  13.8 us (4%)
  other arithmetic  5.23 us (1%)
    reduce_scatter x1, waiting for transfers between devices, local(): lax.psum_scatter(updated, 'rep', scatter_dimension=0, tiled=True) / replicas  146 us
    all_gather x1, waiting for transfers between devices, local(): fragment = lax.all_gather(piece, 'rep', axis=0, tiled=True)  72.9 us
    reduce_scatter x1, waiting for transfers between devices, local(): lax.psum_scatter(partial_value.astype(jnp.bfloat16), 'tp', scatter_dimens...  47.3 us
    unnamed x9, local copies, waits for them, and re-layouts  35.8 us
    dot_general x1, matrix products, local(): lax.dot_general(hidden, lax.all_gather(residual, 'tp', axis=0, tiled=True...  24.9 us
    dot_general x1, matrix products, local(): partial_value = jnp.dot(hidden, weight, preferred_element_type=jnp.float32)  13.8 us
    all_gather x1, waiting for transfers between devices, local(): lax.all_gather(residual, 'tp', axis=0, tiled=True)  9.31 us
  transfers between devices with their start and end apart: 4, of which 4 were waited for; matrix products, arithmetic and copies ran while one was open for 8% of the time, Pallas kernels for 0%

commit v1 on v0

v1 whole, which is shorter than its diff:
```python
import functools

import jax
import jax.numpy as jnp
from jax import lax
from jax.experimental import pallas as pl
from jax.experimental.pallas import tpu as pltpu
from jax.sharding import PartitionSpec as P

beta_one = 0.9
beta_two = 0.999
inner_rate = 0.2
decay_rate = 0.1
outer_rate = 0.7
outer_mu = 0.9
adam_eps = 1e-08

MESH = pl.DeviceIdType.MESH
bf16 = jnp.bfloat16
f32 = jnp.float32


def kernel(n, n_tp, C, W, cnt, RB,
           hidden, target, weight, fm, sm, anchor, om,
           frag_out, mom_out,
           h, wv, goal, pv, prx, psum, yrx, res, anch, dl, rrx, frag, m1, m2, af, omv, mv,
           h_sem, w_sem, g_sem, a_sem, o_sem, m_sem, v_sem, out_sem, mo_sem,
           cs, cr, ys, yr, gs, gr, xs, xr, as_, ar, rs, rr, fs, fr):
    m = n_tp // 2
    KA, KB = n // 2, n // 2 - 1
    me = lax.axis_index("rep")
    tp = lax.axis_index("tp")
    core = lax.rem(tp, 2)
    chip = tp // 2
    mate = tp + 1 - 2 * core
    zz = me // 2
    pos = jnp.where(lax.rem(me, 2) == 0, zz, n - 1 - zz)

    def at_pos(p):
        p = lax.rem(p + 2 * n, n)
        return jnp.where(p < n // 2, 2 * p, 2 * (n - 1 - p) + 1)

    def peer(j):
        return lax.rem(chip + j, m) * 2 + core

    def cols(c):
        return pl.ds(pl.multiple_of(c * W, W), W)

    def h_copy(i):
        return pltpu.make_async_copy(hidden.at[pl.ds(i * cnt, cnt)], h.at[pl.ds(i * cnt, cnt)], h_sem.at[i])

    def w_copy(c):
        return pltpu.make_async_copy(weight.at[0, :, cols(c)], wv.at[c], w_sem.at[c])

    def goal_copy():
        return pltpu.make_async_copy(target.at[pl.ds(pl.multiple_of(tp * cnt, cnt), cnt)], goal, g_sem)

    def a_copy(c):
        return pltpu.make_async_copy(anchor.at[0, :, cols(c)], af.at[c], a_sem.at[c])

    def o_copy(c):
        return pltpu.make_async_copy(om.at[0, :, cols(c)], omv.at[c], o_sem.at[c])

    def m_copy(c, s):
        return pltpu.make_async_copy(fm.at[0, :, cols(c)], m1.at[s], m_sem.at[s])

    def v_copy(c, s):
        return pltpu.make_async_copy(sm.at[0, :, cols(c)], m2.at[s], v_sem.at[s])

    def out_copy(c, b):
        return pltpu.make_async_copy(
            frag.at[c, b], frag_out.at[pl.ds(pl.multiple_of(b * RB, RB), RB), cols(c)], out_sem.at[c, b])

    def mo_copy(c):
        return pltpu.make_async_copy(mv.at[c], mom_out.at[0, :, cols(c)], mo_sem.at[c])

    def remote(src, dst, ss, rsem, dev):
        return pltpu.make_async_remote_copy(
            src_ref=src, dst_ref=dst, send_sem=ss, recv_sem=rsem, device_id=dev, device_id_type=MESH)

    def core_copy(c):
        return remote(pv.at[c, :, 1 - core], prx.at[c], cs.at[c], cr.at[c], {"tp": mate})

    def y_copy(c, j):
        return remote(psum.at[c, j - 1], yrx.at[c, j - 1], ys.at[c, j - 1], yr.at[c, j - 1], {"tp": peer(j)})

    def g_copy(c, j):
        return remote(res.at[c, tp], res.at[c, tp], gs.at[c, j - 1], gr.at[c, j - 1], {"tp": peer(j)})

    def x_copy(c, j):
        src = lax.rem(chip + m - j, m) * 2 + core
        return remote(res.at[c, src], res.at[c, src], xs.at[c, j], xr.at[c, j], {"tp": mate})

    def x_recv(c, j):
        src = lax.rem(chip + m - j, m) * 2 + 1 - core
        return remote(res.at[c, src], res.at[c, src], xs.at[c, j], xr.at[c, j], {"tp": mate})

    def g_recv(c, j):
        src = lax.rem(chip + m - j, m) * 2 + core
        return remote(res.at[c, src], res.at[c, src], gs.at[c, j - 1], gr.at[c, j - 1], {"tp": peer(j)})

    def way(c, side):
        d = 1 - 2 * lax.rem(c, 2)
        return d if side == 0 else -d

    def hops(side):
        return KA if side == 0 else KB

    def slot(side, k):
        return k - 1 if side == 0 else KA + k - 1

    def gather(buf, ss, rsem, c, side, k, recv=False):
        d = way(c, side)
        b = at_pos(pos - d * (k if recv else k - 1))
        i = slot(side, k)
        return remote(buf.at[c, b], buf.at[c, b], ss.at[c, i], rsem.at[c, i], {"rep": at_pos(pos + d)})

    def scatter(c, side, k):
        d = way(c, side)
        b = at_pos(pos + d * (hops(side) - k + 1))
        i = slot(side, k)
        return remote(dl.at[c, b], rrx.at[c, i], rs.at[c, i], rr.at[c, i], {"rep": at_pos(pos + d)})

    for c in range(C):
        a_copy(c).start()
    w_copy(0).start()
    for i in range(n_tp):
        h_copy(i).start()
    goal_copy().start()
    for c in range(1, C):
        w_copy(c).start()
    for s in range(2):
        m_copy(s, s).start()
        v_copy(s, s).start()
    for c in range(C):
        o_copy(c).start()

    barrier = pltpu.get_barrier_semaphore()
    pl.semaphore_signal(barrier, inc=1, device_id={"tp": mate}, device_id_type=MESH)
    for j in range(1, m):
        pl.semaphore_signal(barrier, inc=1, device_id={"tp": peer(j)}, device_id_type=MESH)
    for d in (1, -1):
        pl.semaphore_signal(barrier, inc=1, device_id={"rep": at_pos(pos + d)}, device_id_type=MESH)
    for c in range(C):
        a_copy(c).wait()
        anch[c, me] = af[c].astype(bf16)
    pl.semaphore_wait(barrier, m + 2)

    def anchor_first(c):
        gather(anch, as_, ar, c, 0, 1).start()
        gather(anch, as_, ar, c, 1, 1).start()

    def anchor_hop(k, c):
        for side in (0, 1):
            if k <= hops(side):
                gather(anch, as_, ar, c, side, k, True).wait_recv()
                if k < hops(side):
                    gather(anch, as_, ar, c, side, k + 1).start()

    def forward(c):
        w_copy(c).wait()

        def tile(i, carry):
            @pl.when(c == 0)
            def _():
                h_copy(i).wait()
            pv[c, i // 2, lax.rem(i, 2)] = jnp.dot(
                h[pl.ds(pl.multiple_of(i * cnt, cnt), cnt)], wv[c], preferred_element_type=f32).astype(bf16)
            return carry
        lax.fori_loop(0, n_tp, tile, 0)
        core_copy(c).start()

    def pair(c, to):
        return pv[c, to, core].astype(f32) + prx[c, to].astype(f32)

    def chip_sum(c):
        core_copy(c).wait_recv()
        for j in range(1, m):
            psum[c, j - 1] = pair(c, lax.rem(chip + j, m)).astype(bf16)
            y_copy(c, j).start()

    def residual(c):
        @pl.when(c == 0)
        def _():
            goal_copy().wait()
        total = pair(c, chip)
        for j in range(1, m):
            y_copy(c, j).wait_recv()
            total += yrx[c, j - 1].astype(f32)
        res[c, tp] = (total - goal[:, cols(c)].astype(f32)).astype(bf16)
        for j in range(1, m):
            g_copy(c, j).start()
        x_copy(c, 0).start()

    def spread(c):
        for j in range(1, m):
            g_recv(c, j).wait_recv()
            x_copy(c, j).start()

    GB = max(RB, 128)
    sub = GB // RB
    corr_one = 1.0 - beta_one**3
    corr_two = 1.0 - beta_two**3

    def block(c, i):
        d = way(c, 0)
        half = i // 2
        step = jnp.where(lax.rem(i, 2) == 0, d * (KA - half), -d * (KB - half))
        b = at_pos(pos + step)
        s = lax.rem(c, 2)
        hs = h[:, pl.ds(pl.multiple_of((b // sub) * GB, GB), GB)]
        g = lax.dot_general(hs, res[c].reshape(n_tp * cnt, W), (((0,), (0,)), ((), ())),
                            preferred_element_type=f32)
        if sub > 1:
            part = g[:RB]
            for q in range(1, sub):
                part = jnp.where(lax.rem(b, sub) == q, g[q * RB:(q + 1) * RB], part)
            g = part
        rows = pl.ds(pl.multiple_of(b * RB, RB), RB)
        one = beta_one * m1[s, rows] + (1.0 - beta_one) * g
        two = beta_two * m2[s, rows] + (1.0 - beta_two) * g * g
        wf = wv[c, rows].astype(f32)
        direction = one * (1.0 / corr_one) / (jnp.sqrt(two * (1.0 / corr_two)) + adam_eps)
        updated = wf - inner_rate * (direction + decay_rate * wf)
        dl[c, b] = (anch[c, b].astype(f32) - updated).astype(bf16)

    Q = n // 2

    def inner(c, j):
        s = lax.rem(c, 2)

        @pl.when(j == 0)
        def _():
            for q in range(m):
                x_recv(c, q).wait_recv()
            m_copy(c, s).wait()
            v_copy(c, s).wait()

        def two_blocks(i, carry):
            block(c, j * 2 + i)
            return carry
        lax.fori_loop(0, 2, two_blocks, 0)

        @pl.when(j == 0)
        def _():
            scatter(c, 0, 1).start()
            scatter(c, 1, 1).start()

        @pl.when((j == Q - 1) & (c + 2 < C))
        def _():
            m_copy(c + 2, s).start()
            v_copy(c + 2, s).start()

    def reduce_hop(k, c):
        for side in (0, 1):
            if k <= hops(side):
                scatter(c, side, k).wait_recv()
                if k < hops(side):
                    b = at_pos(pos + way(c, side) * (hops(side) - k))
                    dl[c, b] = (dl[c, b].astype(f32) + rrx[c, slot(side, k)].astype(f32)).astype(bf16)
                    scatter(c, side, k + 1).start()

    def outer(c):
        reduce_hop(KA, c)
        o_copy(c).wait()
        total = dl[c, me].astype(f32) + rrx[c, slot(0, KA)].astype(f32) + rrx[c, slot(1, KB)].astype(f32)
        base = af[c]
        delta = (base - anch[c, me].astype(f32)) + total * (1.0 / n)
        new = outer_mu * omv[c] + delta
        mv[c] = new
        frag[c, me] = (base - outer_rate * (delta + outer_mu * new)).astype(bf16)
        gather(frag, fs, fr, c, 0, 1).start()
        gather(frag, fs, fr, c, 1, 1).start()
        mo_copy(c).start()
        out_copy(c, me).start()

    def frag_hop(k, c):
        for side in (0, 1):
            if k <= hops(side):
                gather(frag, fs, fr, c, side, k, True).wait_recv()
                if k < hops(side):
                    gather(frag, fs, fr, c, side, k + 1).start()
                out_copy(c, at_pos(pos - way(c, side) * k)).start()

    stages = []
    S = Q
    start = 4
    for k in range(1, KA + 1):
        stages.append((k, 2, functools.partial(anchor_hop, k)))
    stages.append((0, 2, anchor_first))
    HS = 1
    for k in range(1, KA):
        stages.append((start + 1 + HS * k, S, functools.partial(reduce_hop, k)))
    last = max(start + 1 + HS * KA, start + Q)
    stages.append((last, S, outer))
    for k in range(1, KA + 1):
        stages.append((last + HS * k, S, functools.partial(frag_hop, k)))
    stages.append((3, S, spread))
    stages.append((2, S, residual))
    stages.append((1, S, chip_sum))
    stages.append((0, S, forward))

    ticks = max(o + s * (C - 1) for o, s, _ in stages) + 1

    def tick(t, carry):
        for off, stride, stage in stages:
            q = t - off

            @pl.when((q >= 0) & (lax.rem(q + stride * ticks, stride) == 0) & (q < stride * C))
            def _():
                stage(q // stride)
        q = t - start

        @pl.when((q >= 0) & (q < Q * C))
        def _():
            inner(q // Q, lax.rem(q, Q))
        return carry
    lax.fori_loop(0, ticks, tick, 0)

    def drain(c, carry):
        core_copy(c).wait_send()
        for j in range(1, m):
            y_copy(c, j).wait_send()
            g_copy(c, j).wait_send()
        for j in range(m):
            x_copy(c, j).wait_send()
        for side in (0, 1):
            for k in range(1, hops(side) + 1):
                gather(anch, as_, ar, c, side, k).wait_send()
                scatter(c, side, k).wait_send()
                gather(frag, fs, fr, c, side, k).wait_send()
        mo_copy(c).wait()
        for b in range(n):
            out_copy(c, b).wait()
        return carry
    lax.fori_loop(0, C, drain, 0)


def local(C, hidden, target, inner_weight, first_moment, second_moment, anchor, outer_momentum):
    n, n_tp = lax.axis_size("rep"), lax.axis_size("tp")
    tok, rows = hidden.shape
    kvw = target.shape[1]
    W = kvw // C
    cnt = tok // n_tp
    RB = rows // n
    m = n_tp // 2
    any_ = pl.BlockSpec(memory_space=pl.ANY)
    dma = pltpu.SemaphoreType.DMA
    V = pltpu.VMEM
    scratch = [
        V((tok, rows), bf16), V((C, rows, W), bf16), V((cnt, kvw), bf16),
        V((C, m, 2, cnt, W), bf16), V((C, m, cnt, W), bf16), V((C, m - 1, cnt, W), bf16),
        V((C, m - 1, cnt, W), bf16), V((C, n_tp, cnt, W), bf16),
        V((C, n, RB, W), bf16), V((C, n, RB, W), bf16), V((C, n - 1, RB, W), bf16), V((C, n, RB, W), bf16),
        V((2, rows, W), f32), V((2, rows, W), f32),
        V((C, RB, W), f32), V((C, RB, W), f32), V((C, RB, W), f32),
        dma((n_tp,)), dma((C,)), dma, dma((C,)), dma((C,)), dma((2,)), dma((2,)), dma((C, n)), dma((C,)),
        dma((C,)), dma((C,)), dma((C, m - 1)), dma((C, m - 1)), dma((C, m - 1)), dma((C, m - 1)),
        dma((C, m)), dma((C, m)),
        dma((C, n - 1)), dma((C, n - 1)), dma((C, n - 1)), dma((C, n - 1)), dma((C, n - 1)), dma((C, n - 1)),
    ]
    return pl.pallas_call(
        functools.partial(kernel, n, n_tp, C, W, cnt, RB),
        out_shape=(jax.ShapeDtypeStruct((rows, kvw), bf16),
                   jax.ShapeDtypeStruct(anchor.shape, f32)),
        in_specs=[any_] * 7,
        out_specs=(any_, any_),
        scratch_shapes=scratch,
        compiler_params=pltpu.CompilerParams(
            collective_id=0, has_side_effects=True, vmem_limit_bytes=62 * 2**20),
        cost_estimate=pl.CostEstimate(
            flops=4 * tok * rows * kvw, bytes_accessed=40 * 2**20, transcendentals=rows * kvw),
    )(hidden, target, inner_weight, first_moment, second_moment, anchor, outer_momentum)


def solution(mesh):
    placed = (
        P("rep", "tp"),
        P("rep", None),
        P("rep", "tp", None),
        P("rep", "tp", None),
        P("rep", "tp", None),
        P("tp", "rep", None),
        P("tp", "rep", None),
    )
    return jax.shard_map(
        functools.partial(local, 4),
        mesh=mesh,
        in_specs=placed,
        out_specs=(P("tp", None), P("tp", "rep", None)),
        check_vma=False,
    )
```

time: 371 us -> 159 us (0.43)
  waiting for transfers between devices: 276 us -> 0 us
  Pallas kernels: 0 us -> 153 us
  matrix products: 38.6 us -> 0 us
  local copies, waits for them, and re-layouts: 35.8 us -> 5.7 us
  between operations: 13.8 us -> 0.65 us
  other arithmetic: 5.23 us -> 0 us
    reduce_scatter x2 -> x0, waiting for transfers between devices: 194 us -> none  [the longest x1 146 us: local(): lax.psum_scatter(updated, 'rep', scatter_dimension=0, tiled=True) / replicas]
    pallas_call x0 -> x1, Pallas kernels: none -> 153 us  [local(): pl.pallas_call(functools.partial(kernel, n, n_tp, C, W, cnt, RB), out_sha...]
    all_gather x2 -> x0, waiting for transfers between devices: 82.2 us -> none  [the longest x1 72.9 us: local(): fragment = lax.all_gather(piece, 'rep', axis=0, tiled=True)]
    dot_general x2 -> x0, matrix products: 38.6 us -> none  [the longest x1 24.9 us: local(): lax.dot_general(hidden, lax.all_gather(residual, 'tp', axis=0, tiled=True...]
    unnamed x9 -> x4, local copies, waits for them, and re-layouts: 35.8 us -> 5.7 us
  transfers between devices with their start and end apart: 4 -> 0, of which waited for: 4 -> 0; matrix products, arithmetic and copies ran while one was open for 8% -> 0% of each run, Pallas kernels for 0% -> 0%
where the time goes in v1:
time: 159 us
  Pallas kernels  153 us (96%)
  local copies, waits for them, and re-layouts  5.7 us (4%)
    pallas_call x1, Pallas kernels, local(): pl.pallas_call(functools.partial(kernel, n, n_tp, C, W, cnt, RB), out_sha...  153 us
    unnamed x4, local copies, waits for them, and re-layouts  5.7 us

profile of v1, /device:TPU:0, one launch (start us, length us, event | category | flops | bytes accessed | tf_op | source)
XLA Modules:
  0.0 159.3 jit_solution(11092782545796294331)
XLA Ops:
  0.6 152.9 %shard_map.86 = (bf16[2048,1024]{1,0:T(8,128)(2,1)}, f32[1,256,1024]{2,1,0:T(8,128)}) custom-call(bf16[2048,2048]{1,0:T(8,128)(2,1)} %hidden.1, bf16[2048,1024]{1,0:T(8,128)(2,1)} %target.1, bf16[1,2048,1024]{2,1,0:T(8,128)(2,1)} %weight.1, f32[1,2048,1024]{2,1,0:T(8,128)} %fm.1, f32[1,2048,1024]{2,1,0:T(8,128)} %sm.1, f32[1,256,1024]{2,1,0:T(8,128)} %anchor.1, ...), custom_call_target="tpu_custom_call" | custom-call | flops 17179869184 | bytes 41943040 | tf_op jit(solution)/shard_map/pallas_call | solution.py:362
  153.6 0.0 copy-start
  153.6 4.7 %copy.11 = bf16[2048,1024]{1,0:T(8,128)(2,1)} copy(bf16[2048,1024]{1,0:T(8,128)(2,1)} %get-tuple-element.4) | data formatting | bytes 8388608
  158.3 0.0 copy-done
  158.3 1.0 copy.12
Async XLA Ops:
  153.6 4.7 %copy-start = (f32[1,256,1024]{2,1,0:T(8,128)S(1)}, f32[1,256,1024]{2,1,0:T(8,128)}, u32[]{:S(2)}) copy-start(f32[1,256,1024]{2,1,0:T(8,128)} %get-tuple-element.5) | copy-start | bytes 3145732

commit v2 on v1

--- a/solution.py
+++ b/solution.py
@@ -201,6 +201,7 @@
     sub = GB // RB
     corr_one = 1.0 - beta_one**3
     corr_two = 1.0 - beta_two**3
+    keep = 1.0 - inner_rate * decay_rate
 
     def block(c, i):
         d = way(c, 0)
@@ -222,9 +223,11 @@
         wf = wv[c, rows].astype(f32)
         direction = one * (1.0 / corr_one) / (jnp.sqrt(two * (1.0 / corr_two)) + adam_eps)
         updated = wf - inner_rate * (direction + decay_rate * wf)
-        dl[c, b] = (anch[c, b].astype(f32) - updated).astype(bf16)
+        dl[c, b] = (keep * anch[c, b].astype(f32) - updated).astype(bf16)
 
     Q = n // 2
+    parts = 1
+    size = n // parts
 
     def inner(c, j):
         s = lax.rem(c, 2)
@@ -236,17 +239,20 @@
             m_copy(c, s).wait()
             v_copy(c, s).wait()
 
-        def two_blocks(i, carry):
-            block(c, j * 2 + i)
+        def one_block(i, carry):
+            block(c, j * size + i)
+
+            @pl.when((j == 0) & (i == 0))
+            def _():
+                scatter(c, 0, 1).start()
+
+            @pl.when((j == 0) & (i == 1))
+            def _():
+                scatter(c, 1, 1).start()
             return carry
-        lax.fori_loop(0, 2, two_blocks, 0)
-
-        @pl.when(j == 0)
-        def _():
-            scatter(c, 0, 1).start()
-            scatter(c, 1, 1).start()
-
-        @pl.when((j == Q - 1) & (c + 2 < C))
+        lax.fori_loop(0, size, one_block, 0)
+
+        @pl.when((j == parts - 1) & (c + 2 < C))
         def _():
             m_copy(c + 2, s).start()
             v_copy(c + 2, s).start()
@@ -265,7 +271,7 @@
         o_copy(c).wait()
         total = dl[c, me].astype(f32) + rrx[c, slot(0, KA)].astype(f32) + rrx[c, slot(1, KB)].astype(f32)
         base = af[c]
-        delta = (base - anch[c, me].astype(f32)) + total * (1.0 / n)
+        delta = (base - keep * anch[c, me].astype(f32)) + total * (1.0 / n)
         new = outer_mu * omv[c] + delta
         mv[c] = new
         frag[c, me] = (base - outer_rate * (delta + outer_mu * new)).astype(bf16)
@@ -282,23 +288,20 @@
                     gather(frag, fs, fr, c, side, k + 1).start()
                 out_copy(c, at_pos(pos - way(c, side) * k)).start()
 
-    stages = []
-    S = Q
-    start = 4
-    for k in range(1, KA + 1):
-        stages.append((k, 2, functools.partial(anchor_hop, k)))
-    stages.append((0, 2, anchor_first))
-    HS = 1
-    for k in range(1, KA):
-        stages.append((start + 1 + HS * k, S, functools.partial(reduce_hop, k)))
-    last = max(start + 1 + HS * KA, start + Q)
-    stages.append((last, S, outer))
-    for k in range(1, KA + 1):
-        stages.append((last + HS * k, S, functools.partial(frag_hop, k)))
-    stages.append((3, S, spread))
-    stages.append((2, S, residual))
-    stages.append((1, S, chip_sum))
-    stages.append((0, S, forward))
+    S = parts
+    start = max(4, KA)
+
+    def after(k):
+        return start + 1 + max(k - 1, min(k, Q - 1) * parts // Q)
+
+    tp_stages = [(3, S, spread), (2, S, residual), (1, S, chip_sum), (0, S, forward)]
+    stages = [(k, S, functools.partial(anchor_hop, k)) for k in range(1, KA + 1)]
+    stages += [(0, S, anchor_first)]
+    ring = [(after(k), S, functools.partial(reduce_hop, k)) for k in range(1, KA)]
+    last = after(KA)
+    ring += [(last, S, outer)]
+    ring += [(last + k, S, functools.partial(frag_hop, k)) for k in range(1, KA + 1)]
+    stages = tp_stages[::-1] + stages + ring
 
     ticks = max(o + s * (C - 1) for o, s, _ in stages) + 1
 
@@ -311,9 +314,9 @@
                 stage(q // stride)
         q = t - start
 
-        @pl.when((q >= 0) & (q < Q * C))
+        @pl.when((q >= 0) & (q < parts * C))
         def _():
-            inner(q // Q, lax.rem(q, Q))
+            inner(q // parts, lax.rem(q, parts))
         return carry
     lax.fori_loop(0, ticks, tick, 0)
 

time: 159 us -> 151 us (0.950)
  Pallas kernels: 153 us -> 144 us
    pallas_call x1, Pallas kernels: 153 us -> 144 us  [local(): pl.pallas_call(functools.partial(kernel, n, n_tp, C, W, cnt, RB), out_sha...]
where the time goes in v2:
time: 151 us
  Pallas kernels  144 us (95%)
  local copies, waits for them, and re-layouts  5.7 us (4%)
    pallas_call x1, Pallas kernels, local(): pl.pallas_call(functools.partial(kernel, n, n_tp, C, W, cnt, RB), out_sha...  144 us
    unnamed x4, local copies, waits for them, and re-layouts  5.7 us

profile of v2, /device:TPU:0, one launch (start us, length us, event | category | flops | bytes accessed | tf_op | source)
XLA Modules:
  0.0 150.6 jit_solution(1167441215450527370)
XLA Ops:
  0.6 144.2 %shard_map.86 = (bf16[2048,1024]{1,0:T(8,128)(2,1)}, f32[1,256,1024]{2,1,0:T(8,128)}) custom-call(bf16[2048,2048]{1,0:T(8,128)(2,1)} %hidden.1, bf16[2048,1024]{1,0:T(8,128)(2,1)} %target.1, bf16[1,2048,1024]{2,1,0:T(8,128)(2,1)} %weight.1, f32[1,2048,1024]{2,1,0:T(8,128)} %fm.1, f32[1,2048,1024]{2,1,0:T(8,128)} %sm.1, f32[1,256,1024]{2,1,0:T(8,128)} %anchor.1, ...), custom_call_target="tpu_custom_call" | custom-call | flops 17179869184 | bytes 41943040 | tf_op jit(solution)/shard_map/pallas_call | solution.py:365
  144.9 0.0 copy-start
  144.9 4.7 %copy.11 = bf16[2048,1024]{1,0:T(8,128)(2,1)} copy(bf16[2048,1024]{1,0:T(8,128)(2,1)} %get-tuple-element.4) | data formatting | bytes 8388608
  149.6 0.0 copy-done
  149.6 1.0 copy.12
Async XLA Ops:
  144.9 4.7 %copy-start = (f32[1,256,1024]{2,1,0:T(8,128)S(1)}, f32[1,256,1024]{2,1,0:T(8,128)}, u32[]{:S(2)}) copy-start(f32[1,256,1024]{2,1,0:T(8,128)} %get-tuple-element.5) | copy-start | bytes 3145732
